TPU v7x, 128 devices: a whole 4x4x4 slice. The times are simulated.
128 devices in a mesh: dom: 16 (over z, y), sub: 8 (over x, core).
Axes of the slice: x: 4, y: 4, z: 4, core: 2. Of those that a mesh axis runs over, the one named last changes fastest.
Arguments:
- embeddings: float32 [262144, 400], P(('dom', 'sub')), may hold values from -5 to 5
- adagrad_state: float32 [262144], P(('dom', 'sub')), may hold values from 0.01 to 0.1
- relations: float32 [7424, 400], replicated, may hold values from 0.5 to 2
- pairing: int32 [2], replicated, may hold values from 1 to 15, as said below
- row_lists: int32 [2, 32768], P(None, ('dom', 'sub')), may hold values from 0 to 2047, as said below
- row_counts: int32 [2, 128], P(None, ('dom', 'sub')), may hold values from 1 to 256, as said below
- group_counts: int32 [2, 128], P(None, ('dom', 'sub')), may hold values from 1 to 3, as said below
- head_ids: int32 [2, 384000], P(None, ('dom', 'sub')), may hold values from 0 to 2047
- relation_ids: int32 [2, 384000], P(None, ('dom', 'sub')), may hold values from 0 to 7423
- tail_slots: int32 [2, 384000], P(None, ('dom', 'sub')), may hold values from 0 to 2047, as said below
- negatives: int32 [2, 384000], P(None, ('dom', 'sub')), may hold values from 0 to 2047, as said below
Outputs:
- new_embeddings: float32 [262144, 400], P(('dom', 'sub'))
- new_state: float32 [262144], P(('dom', 'sub'))
Inputs may be any that keep to these rules, and one draw needn't show every extreme that they name: pairing[r] is the partner mask of round r; in some round it is 16 - 1. `row_lists`: the entries of one device's list in one round are distinct local row ids; entries from slot row_counts on are ignored. `row_counts`: in each round some device's list is full. `group_counts`: in each round some device uses all 3 edge group slots. `tail_slots`: A slot s' * 256 + k names slot k of the list of the partner device with sub index s', and k is below that list's count in that round. `negatives`: as for tail_slots.
All inputs are finite; a program needn't handle non-finite values.
Results may differ from a plain program's by a relative error of at most 0.0003.
Values sent between devices are 32-bit elements; how exact they have to be, the bound alone decides.
A program may use at most 192 MiB of HBM per device.

v0:
```python
import jax
import jax.numpy as jnp
from jax import lax
from jax.sharding import PartitionSpec as P

GROUP = 1000
NNEG = 1000


exact_mode = lax.Precision.HIGHEST
learn_rate = 0.1


def partner_2(block, axis, stride):
    count = lax.axis_size(axis)
    route = []
    for low in range(count):
        high = low | 1 << stride
        if high != low and high < count:
            route += [(low, high), (high, low)]
    return lax.ppermute(block, axis, route)


def group_terms(
    own_rows, partner_block, relations, head_part, relation_part, tail_part, negative_part, active
):
    head_rows = own_rows[head_part]
    scale_rows = relations[relation_part]
    queries = head_rows * scale_rows
    tail_rows = partner_block[tail_part]
    negative_rows = partner_block[negative_part]
    positive = jnp.sum(queries * tail_rows, axis=1)
    negative = jnp.dot(
        queries, negative_rows.T, precision=exact_mode, preferred_element_type=jnp.float32
    )
    highest = jnp.maximum(jnp.max(negative, axis=1), positive)
    pos_weight = jnp.exp(positive - highest)
    neg_weight = jnp.exp(negative - highest[:, None])
    totals = pos_weight + jnp.sum(neg_weight, axis=1)
    pos_share = pos_weight / totals * active - active
    neg_share = neg_weight / totals[:, None] * active
    query_grad = pos_share[:, None] * tail_rows + jnp.dot(
        neg_share, negative_rows, precision=exact_mode, preferred_element_type=jnp.float32
    )
    negative_grad = jnp.dot(
        neg_share.T, queries, precision=exact_mode, preferred_element_type=jnp.float32
    )
    return (query_grad * scale_rows, pos_share[:, None] * queries, negative_grad)


def send_rows(values, partner_mask):
    current = values
    for bit_number in range(lax.axis_size("dom").bit_length() - 1):
        take_swapped = jnp.bitwise_and(jnp.right_shift(partner_mask, bit_number), 1) == 1
        current = lax.cond(
            take_swapped,
            lambda held: partner_2(held, "dom", bit_number),
            lambda held: held,
            current,
        )
    return current


def send_grads(values, partner_mask):
    current = values
    for bit_number in range(lax.axis_size("dom").bit_length() - 1):
        take_swapped = jnp.bitwise_and(jnp.right_shift(partner_mask, bit_number), 1) == 1
        current = lax.cond(
            take_swapped,
            lambda held: partner_2(held, "dom", bit_number),
            lambda held: held,
            current,
        )
    return current


def body(
    embeddings,
    adagrad_state,
    relations,
    pairing,
    row_lists,
    row_counts,
    group_counts,
    head_ids,
    relation_ids,
    tail_slots,
    negatives,
):
    list_rows = row_lists.shape[1]
    for round_number in range(pairing.shape[0]):
        partner_mask = pairing[round_number]
        row_ids = row_lists[round_number]
        filled = jnp.arange(list_rows, dtype=jnp.int32) < row_counts[round_number, 0]
        outgoing = jnp.where(filled[:, None], embeddings[row_ids], 0.0)
        incoming = send_rows(outgoing, partner_mask)
        partner_block = lax.all_gather(incoming, "sub", axis=0, tiled=True)
        head_all = head_ids[round_number]
        relation_all = relation_ids[round_number]
        tail_all = tail_slots[round_number]
        negative_all = negatives[round_number]
        own_rows = embeddings

        def step(group_index, sums_carry):
            rows_grad, block_grad = sums_carry
            first = group_index * GROUP
            head_part = lax.dynamic_slice_in_dim(head_all, first, GROUP)
            relation_part = lax.dynamic_slice_in_dim(relation_all, first, GROUP)
            tail_part = lax.dynamic_slice_in_dim(tail_all, first, GROUP)
            negative_part = lax.dynamic_slice_in_dim(negative_all, group_index * NNEG, NNEG)
            head_grad, tail_grad, negative_grad = group_terms(
                own_rows,
                partner_block,
                relations,
                head_part,
                relation_part,
                tail_part,
                negative_part,
                jnp.float32(1.0),
            )
            rows_grad = rows_grad.at[head_part].add(head_grad)
            block_grad = (
                block_grad.at[tail_part].add(tail_grad).at[negative_part].add(negative_grad)
            )
            return (rows_grad, block_grad)

        empty_rows = jnp.zeros(embeddings.shape, jnp.float32)
        empty_block = jnp.zeros(partner_block.shape, jnp.float32)
        rows_grad, block_grad = lax.fori_loop(
            0, group_counts[round_number, 0], step, (empty_rows, empty_block)
        )
        own_share = lax.psum_scatter(block_grad, "sub", scatter_dimension=0, tiled=True)
        returned = send_grads(own_share, partner_mask)
        returned = jnp.where(filled[:, None], returned, 0.0)
        totals = rows_grad.at[row_ids].add(returned)
        adagrad_state = adagrad_state + jnp.mean(totals * totals, axis=1)
        embeddings = embeddings - learn_rate * totals / jnp.sqrt(adagrad_state)[:, None]
    return (embeddings, adagrad_state)


def solution(mesh):
    in_specs = (
        P(("dom", "sub"), None),
        P(("dom", "sub")),
        P(),
        P(),
        P(None, ("dom", "sub")),
        P(None, ("dom", "sub")),
        P(None, ("dom", "sub")),
        P(None, ("dom", "sub")),
        P(None, ("dom", "sub")),
        P(None, ("dom", "sub")),
        P(None, ("dom", "sub")),
    )
    out_specs = (P(("dom", "sub"), None), P(("dom", "sub")))
    return jax.shard_map(body, mesh=mesh, in_specs=in_specs, out_specs=out_specs, check_vma=False)
```

profile of v0, /device:TPU:96, one launch (start us, length us, event | category | flops | bytes accessed | tf_op | source)
XLA Modules:
  0.0 1058.9 jit_solution(5652376453513218175)
XLA Ops:
  20.8 13.8 %conditional.16 = (f32[256,400]{1,0:T(8,128)S(1)}) conditional(s32[]{:T(128)} %bitcast.7, f32[256,400]{1,0:T(8,128)S(1)} %broadcast_select_fusion.1, f32[256,400]{1,0:T(8,128)S(1)} %broadcast_select_fusion.1), branch_computations={%region_0.1_spmd, %region_1.2_spmd} | conditional | bytes 2457648 | solution.py:55
  22.5 12.1 %collective-permute-done = f32[256,400]{1,0:T(8,128)S(1)} collective-permute-done((f32[256,400]{1,0:T(8,128)S(1)}, f32[256,400]{1,0:T(8,128)S(1)}, u32[]{:S(2)}, u32[]{:S(2)}) %collective-permute-start) | collective-permute-done | bytes 409632 | tf_op jit(solution)/shard_map/cond/branch_1_fun/ppermute | solution.py:21
  34.6 13.4 %conditional.18 = (f32[256,400]{1,0:T(8,128)S(1)}) conditional(s32[]{:T(128)} %bitcast.5, f32[256,400]{1,0:T(8,128)S(1)} %get-tuple-element.765, f32[256,400]{1,0:T(8,128)S(1)} %get-tuple-element.765), branch_computations={%region_4.5_spmd, %region_5.6_spmd} | conditional | bytes 2457648 | solution.py:55
  35.1 12.9 %collective-permute-done.2 = f32[256,400]{1,0:T(8,128)S(1)} collective-permute-done((f32[256,400]{1,0:T(8,128)S(1)}, f32[256,400]{1,0:T(8,128)S(1)}, u32[]{:S(2)}, u32[]{:S(2)}) %collective-permute-start.2) | collective-permute-done | bytes 409632 | tf_op jit(solution)/shard_map/cond/branch_1_fun/ppermute | solution.py:21
  48.1 13.0 %conditional.19 = (f32[256,400]{1,0:T(8,128)S(1)}) conditional(s32[]{:T(128)} %bitcast.4, f32[256,400]{1,0:T(8,128)S(1)} %get-tuple-element.766, f32[256,400]{1,0:T(8,128)S(1)} %get-tuple-element.766), branch_computations={%region_6.7_spmd, %region_7.8_spmd} | conditional | bytes 2457648 | solution.py:55
  48.2 12.8 %collective-permute-done.3 = f32[256,400]{1,0:T(8,128)S(1)} collective-permute-done((f32[256,400]{1,0:T(8,128)S(1)}, f32[256,400]{1,0:T(8,128)S(1)}, u32[]{:S(2)}, u32[]{:S(2)}) %collective-permute-start.3) | collective-permute-done | bytes 409632 | tf_op jit(solution)/shard_map/cond/branch_1_fun/ppermute | solution.py:21
  62.0 14.3 %copy.47 = f32[7424,400]{1,0:T(8,128)} copy(f32[7424,400]{0,1:T(8,128)} %param.49) | data formatting | bytes 23756800 | tf_op jit(solution)/shard_map/while | solution.py:129
  79.4 16.0 %all-gather.3.cloned.1.call-done = f32[2048,400]{1,0:T(8,128)} async-done(((f32[256,400]{1,0:T(8,128)}), f32[2048,400]{1,0:T(8,128)}) %all-gather.3.cloned.1.call-update) | async-done | bytes 3276816 | tf_op jit(solution)/shard_map/all_gather | solution.py:97
  100.6 109.9 %while.28 = (s32[]{:T(128)}, f32[2048,400]{1,0:T(8,128)}, f32[2048,400]{1,0:T(8,128)}, s32[]{:T(128)}, s32[3000]{0:T(1024)S(1)}, /*index=5*/f32[2048,400]{1,0:T(...) while((s32[]{:T(128)}, f32[2048,400]{1,0:T(8,128)}, ...), condition=%wide.region_15.16_spmd, body=%wide.region_8.15_spmd.sunk | while | flops 14411019264 | bytes 116964696 | solution.py:129
  101.6 9.5 gather_fusion
  121.1 7.4 gather_fusion.2
  139.7 7.2 fusion.63
  158.4 11.5 %scatter_fusion = f32[2048,400]{1,0:T(8,128)} fusion(f32[2048,400]{1,0:T(8,128)} %get-tuple-element.690, s32[1000]{0:T(1024)S(1)} %get-tuple-element.643, f32[1000,400]{1,0:T(8,128)} %copy.66), kind=kCustom, calls=%fused_computation.10.clone.1 | custom fusion | flops 400000 | bytes 4804000 | tf_op jit(solution)/shard_map/while/body/scatter-add | solution.py:121
  171.9 11.4 %scatter_fusion.1 = f32[2048,400]{1,0:T(8,128)} fusion(f32[2048,400]{1,0:T(8,128)} %get-tuple-element.691, s32[1000]{0:T(1024)S(1)} %get-tuple-element.645, f32[1000,400]{1,0:T(8,128)} %copy.67), kind=kCustom, calls=%fused_computation.11.clone.1 | custom fusion | flops 400000 | bytes 4804000 | tf_op jit(solution)/shard_map/while/body/scatter-add | solution.py:123
  183.3 9.8 fusion.65
  193.1 11.4 %scatter_fusion.2 = f32[2048,400]{1,0:T(8,128)} fusion(f32[2048,400]{1,0:T(8,128)} %scatter_fusion.1, s32[1000]{0:T(1024)S(1)} %get-tuple-element.646, f32[1000,400]{1,0:T(8,128)} %fusion.65), kind=kCustom, calls=%fused_computation.12.clone.1 | custom fusion | flops 400000 | bytes 4804000 | tf_op jit(solution)/shard_map/while/body/scatter-add | solution.py:123
  213.9 241.8 %reduce-scatter.3.cloned.1.call-done = f32[256,400]{1,0:T(8,128)} async-done(((f32[2048,400]{1,0:T(8,128)}), f32[256,400]{1,0:T(8,128)}) %reduce-scatter.3.cloned.1.call-update) | async-done | bytes 409616 | tf_op jit(solution)/shard_map/reduce_scatter | solution.py:132
  455.7 11.7 %conditional.20 = (f32[256,400]{1,0:T(8,128)}) conditional(s32[]{:T(128)} %bitcast.7, f32[256,400]{1,0:T(8,128)} %reduce-scatter.3.cloned.1.call-done, f32[256,400]{1,0:T(8,128)} %reduce-scatter.3.cloned.1.call-done), branch_computations={%region_17.18_spmd, %region_18.19_spmd} | conditional | bytes 2457648 | solution.py:68
  457.3 9.3 collective-permute-done.4
  467.4 12.7 %conditional.22 = (f32[256,400]{1,0:T(8,128)}) conditional(s32[]{:T(128)} %bitcast.5, f32[256,400]{1,0:T(8,128)} %get-tuple-element.769, f32[256,400]{1,0:T(8,128)} %get-tuple-element.769), branch_computations={%region_21.22_spmd, %region_22.23_spmd} | conditional | bytes 2457648 | solution.py:68
  468.1 11.1 %collective-permute-done.6 = f32[256,400]{1,0:T(8,128)S(1)} collective-permute-done((f32[256,400]{1,0:T(8,128)}, f32[256,400]{1,0:T(8,128)S(1)}, u32[]{:S(2)}, u32[]{:S(2)}) %collective-permute-start.6) | collective-permute-done | bytes 409632 | tf_op jit(solution)/shard_map/cond/branch_1_fun/ppermute | solution.py:21
  480.1 11.7 %conditional.23 = (f32[256,400]{1,0:T(8,128)}) conditional(s32[]{:T(128)} %bitcast.4, f32[256,400]{1,0:T(8,128)} %get-tuple-element.770, f32[256,400]{1,0:T(8,128)} %get-tuple-element.770), branch_computations={%region_23.24_spmd, %region_24.25_spmd} | conditional | bytes 2457648 | solution.py:68
  480.1 10.9 %collective-permute-done.7 = f32[256,400]{1,0:T(8,128)S(1)} collective-permute-done((f32[256,400]{1,0:T(8,128)}, f32[256,400]{1,0:T(8,128)S(1)}, u32[]{:S(2)}, u32[]{:S(2)}) %collective-permute-start.7) | collective-permute-done | bytes 409632 | tf_op jit(solution)/shard_map/cond/branch_1_fun/ppermute | solution.py:21
  510.5 14.3 %conditional.24 = (f32[256,400]{1,0:T(8,128)S(1)}) conditional(s32[]{:T(128)} %bitcast.19, f32[256,400]{1,0:T(8,128)S(1)} %broadcast_select_fusion, f32[256,400]{1,0:T(8,128)S(1)} %broadcast_select_fusion), branch_computations={%region_27.28_spmd, %region_28.29_spmd} | conditional | bytes 2457648 | solution.py:55
  512.6 12.1 %collective-permute-done.8 = f32[256,400]{1,0:T(8,128)S(1)} collective-permute-done((f32[256,400]{1,0:T(8,128)S(1)}, f32[256,400]{1,0:T(8,128)S(1)}, u32[]{:S(2)}, u32[]{:S(2)}) %collective-permute-start.8) | collective-permute-done | bytes 409632 | tf_op jit(solution)/shard_map/cond/branch_1_fun/ppermute | solution.py:21
  524.8 10.9 %conditional.25 = (f32[256,400]{1,0:T(8,128)S(1)}) conditional(s32[]{:T(128)} %bitcast.18, f32[256,400]{1,0:T(8,128)S(1)} %get-tuple-element.772, f32[256,400]{1,0:T(8,128)S(1)} %get-tuple-element.772), branch_computations={%region_29.30_spmd, %region_30.31_spmd} | conditional | bytes 2457648 | solution.py:55
  535.7 13.9 %conditional.26 = (f32[256,400]{1,0:T(8,128)S(1)}) conditional(s32[]{:T(128)} %bitcast.17, f32[256,400]{1,0:T(8,128)S(1)} %get-tuple-element.773, f32[256,400]{1,0:T(8,128)S(1)} %get-tuple-element.773), branch_computations={%region_31.32_spmd, %region_32.33_spmd} | conditional | bytes 2457648 | solution.py:55
  535.8 13.7 %collective-permute-done.10 = f32[256,400]{1,0:T(8,128)S(1)} collective-permute-done((f32[256,400]{1,0:T(8,128)S(1)}, f32[256,400]{1,0:T(8,128)S(1)}, u32[]{:S(2)}, u32[]{:S(2)}) %collective-permute-start.10) | collective-permute-done | bytes 409632 | tf_op jit(solution)/shard_map/cond/branch_1_fun/ppermute | solution.py:21
  549.5 10.8 %conditional.27 = (f32[256,400]{1,0:T(8,128)S(1)}) conditional(s32[]{:T(128)} %bitcast.16, f32[256,400]{1,0:T(8,128)S(1)} %get-tuple-element.774, f32[256,400]{1,0:T(8,128)S(1)} %get-tuple-element.774), branch_computations={%region_33.34_spmd, %region_34.35_spmd} | conditional | bytes 2457648 | solution.py:55
  549.7 10.7 %collective-permute-done.11 = f32[256,400]{1,0:T(8,128)S(1)} collective-permute-done((f32[256,400]{1,0:T(8,128)S(1)}, f32[256,400]{1,0:T(8,128)S(1)}, u32[]{:S(2)}, u32[]{:S(2)}) %collective-permute-start.11) | collective-permute-done | bytes 409632 | tf_op jit(solution)/shard_map/cond/branch_1_fun/ppermute | solution.py:21
  561.2 40.6 %all-gather.5.cloned.1.call-done = f32[2048,400]{1,0:T(8,128)} async-done(((f32[256,400]{1,0:T(8,128)}), f32[2048,400]{1,0:T(8,128)}) %all-gather.5.cloned.1.call-update) | async-done | bytes 3276816 | tf_op jit(solution)/shard_map/all_gather | solution.py:97
  607.0 126.8 %while.29 = (s32[]{:T(128)}, f32[2048,400]{1,0:T(8,128)}, f32[2048,400]{1,0:T(8,128)}, s32[]{:T(128)}, s32[3000]{0:T(1024)}, /*index=5*/f32[2048,400]{1,0:T(8,12...) while((s32[]{:T(128)}, f32[2048,400]{1,0:T(8,128)}, ...), condition=%wide.region_42.43_spmd, body=%wide.region_35.42_spmd.sunk | while | flops 14411019264 | bytes 116964696 | solution.py:129
  629.2 9.5 gather_fusion.4
  649.4 7.4 gather_fusion.6
  668.1 7.2 fusion.72
  686.7 11.5 %scatter_fusion.3 = f32[2048,400]{1,0:T(8,128)} fusion(f32[2048,400]{1,0:T(8,128)} %get-tuple-element.735, s32[1000]{0:T(1024)S(1)} %get-tuple-element.664, f32[1000,400]{1,0:T(8,128)} %copy.71), kind=kCustom, calls=%fused_computation.13.clone.1 | custom fusion | flops 400000 | bytes 4804000 | tf_op jit(solution)/shard_map/while/body/scatter-add | solution.py:121
  700.3 11.4 %scatter_fusion.4 = f32[2048,400]{1,0:T(8,128)} fusion(f32[2048,400]{1,0:T(8,128)} %get-tuple-element.736, s32[1000]{0:T(1024)S(1)} %get-tuple-element.666, f32[1000,400]{1,0:T(8,128)} %copy.72), kind=kCustom, calls=%fused_computation.14.clone.1 | custom fusion | flops 400000 | bytes 4804000 | tf_op jit(solution)/shard_map/while/body/scatter-add | solution.py:123
  711.7 9.8 fusion.74
  721.5 11.4 %scatter_fusion.5 = f32[2048,400]{1,0:T(8,128)} fusion(f32[2048,400]{1,0:T(8,128)} %scatter_fusion.4, s32[1000]{0:T(1024)S(1)} %get-tuple-element.667, f32[1000,400]{1,0:T(8,128)} %fusion.74), kind=kCustom, calls=%fused_computation.15.clone.1 | custom fusion | flops 400000 | bytes 4804000 | tf_op jit(solution)/shard_map/while/body/scatter-add | solution.py:123
  733.8 248.1 %reduce-scatter.5.cloned.1.call-done = f32[256,400]{1,0:T(8,128)} async-done(((f32[2048,400]{1,0:T(8,128)}), f32[256,400]{1,0:T(8,128)}) %reduce-scatter.5.cloned.1.call-update) | async-done | bytes 409616 | tf_op jit(solution)/shard_map/reduce_scatter | solution.py:132
  981.9 11.7 %conditional.28 = (f32[256,400]{1,0:T(8,128)}) conditional(s32[]{:T(128)} %bitcast.19, f32[256,400]{1,0:T(8,128)} %reduce-scatter.5.cloned.1.call-done, f32[256,400]{1,0:T(8,128)} %reduce-scatter.5.cloned.1.call-done), branch_computations={%region_44.45_spmd, %region_45.46_spmd} | conditional | bytes 2457648 | solution.py:68
  983.5 9.4 collective-permute-done.12
  993.7 13.4 %conditional.29 = (f32[256,400]{1,0:T(8,128)}) conditional(s32[]{:T(128)} %bitcast.18, f32[256,400]{1,0:T(8,128)} %get-tuple-element.776, f32[256,400]{1,0:T(8,128)} %get-tuple-element.776), branch_computations={%region_46.47_spmd, %region_47.48_spmd} | conditional | bytes 2457648 | solution.py:68
  996.7 9.6 collective-permute-done.13
  1007.1 12.8 %conditional.30 = (f32[256,400]{1,0:T(8,128)}) conditional(s32[]{:T(128)} %bitcast.17, f32[256,400]{1,0:T(8,128)} %get-tuple-element.777, f32[256,400]{1,0:T(8,128)} %get-tuple-element.777), branch_computations={%region_48.49_spmd, %region_49.50_spmd} | conditional | bytes 2457648 | solution.py:68
  1007.9 11.2 %collective-permute-done.14 = f32[256,400]{1,0:T(8,128)S(1)} collective-permute-done((f32[256,400]{1,0:T(8,128)}, f32[256,400]{1,0:T(8,128)S(1)}, u32[]{:S(2)}, u32[]{:S(2)}) %collective-permute-start.14) | collective-permute-done | bytes 409632 | tf_op jit(solution)/shard_map/cond/branch_1_fun/ppermute | solution.py:21
  1019.9 11.7 %conditional.31 = (f32[256,400]{1,0:T(8,128)}) conditional(s32[]{:T(128)} %bitcast.16, f32[256,400]{1,0:T(8,128)} %get-tuple-element.778, f32[256,400]{1,0:T(8,128)} %get-tuple-element.778), branch_computations={%region_50.51_spmd, %region_51.52_spmd} | conditional | bytes 2457648 | solution.py:68
  1019.9 10.9 %collective-permute-done.15 = f32[256,400]{1,0:T(8,128)S(1)} collective-permute-done((f32[256,400]{1,0:T(8,128)}, f32[256,400]{1,0:T(8,128)S(1)}, u32[]{:S(2)}, u32[]{:S(2)}) %collective-permute-start.15) | collective-permute-done | bytes 409632 | tf_op jit(solution)/shard_map/cond/branch_1_fun/ppermute | solution.py:21
  (167 shorter events, 165.8 us)
Async XLA Ops:
  7.2 5.1 copy-start.27
  7.2 8.3 copy-start.26
  7.2 8.9 copy-start.28
  7.2 88.2 %all-gather.3.cloned.1.call-start = ((), (), s32[]{:S(2)}) async-start(), calls=%async_computation.2 | async-start | bytes 4718592 | tf_op jit(solution)/shard_map/all_gather | solution.py:97
  16.1 0.6 copy-start.21
  17.3 3.5 copy-start.24
  20.8 13.7 %collective-permute-start = (f32[256,400]{1,0:T(8,128)S(1)}, f32[256,400]{1,0:T(8,128)S(1)}, u32[]{:S(2)}, u32[]{:S(2)}) collective-permute-start(f32[256,400]{1,0:T(8,128)S(1)} %param.1), channel_id=1, source_target_pairs={{0,8},{8,0},{16,24},{24,16},{32,40},{40,32},{48,56},{56,48},{64,72... | collective-permute-start | bytes 1228808 | tf_op jit(solution)/shard_map/cond/branch_1_fun/ppermute | solution.py:21
  34.7 13.4 %collective-permute-start.2 = (f32[256,400]{1,0:T(8,128)S(1)}, f32[256,400]{1,0:T(8,128)S(1)}, u32[]{:S(2)}, u32[]{:S(2)}) collective-permute-start(f32[256,400]{1,0:T(8,128)S(1)} %param.5), channel_id=1, source_target_pairs={{0,32},{32,0},{8,40},{40,8},{16,48},{48,16},{24,56},{56,24},{64,96... | collective-permute-start | bytes 1228808 | tf_op jit(solution)/shard_map/cond/branch_1_fun/ppermute | solution.py:21
  48.1 13.0 %collective-permute-start.3 = (f32[256,400]{1,0:T(8,128)S(1)}, f32[256,400]{1,0:T(8,128)S(1)}, u32[]{:S(2)}, u32[]{:S(2)}) collective-permute-start(f32[256,400]{1,0:T(8,128)S(1)} %param.7), channel_id=1, source_target_pairs={{0,64},{64,0},{8,72},{72,8},{16,80},{80,16},{24,88},{88,24},{32,96... | collective-permute-start | bytes 1228808 | tf_op jit(solution)/shard_map/cond/branch_1_fun/ppermute | solution.py:21
  61.1 0.8 copy-start.10
  61.9 393.8 %reduce-scatter.3.cloned.1.call-start = ((), (), s32[]{:S(2)}) async-start(), calls=%async_computation.3 | async-start | bytes 4718592 | tf_op jit(solution)/shard_map/reduce_scatter | solution.py:132
  61.9 14.3 %copy-start.29 = (s32[2,1]{0,1:T(1,128)S(1)}, s32[2,1]{0,1:T(1,128)}, u32[]{:S(2)}) copy-start(s32[2,1]{0,1:T(1,128)} %param.53) | copy-start | bytes 28
  62.0 15.0 %copy-start.16 = (s32[2,3000]{1,0:T(2,128)S(1)}, s32[2,3000]{1,0:T(2,128)}, u32[]{:S(2)}) copy-start(s32[2,3000]{1,0:T(2,128)} %param.54) | copy-start | bytes 72004
  62.0 15.6 %copy-start.17 = (s32[2,3000]{1,0:T(2,128)S(1)}, s32[2,3000]{1,0:T(2,128)}, u32[]{:S(2)}) copy-start(s32[2,3000]{1,0:T(2,128)} %param.55) | copy-start | bytes 72004
  62.0 16.2 %copy-start.18 = (s32[2,3000]{1,0:T(2,128)S(1)}, s32[2,3000]{1,0:T(2,128)}, u32[]{:S(2)}) copy-start(s32[2,3000]{1,0:T(2,128)} %param.56) | copy-start | bytes 72004
  62.0 16.8 %copy-start.19 = (s32[2,3000]{1,0:T(2,128)S(1)}, s32[2,3000]{1,0:T(2,128)}, u32[]{:S(2)}) copy-start(s32[2,3000]{1,0:T(2,128)} %param.57) | copy-start | bytes 72004
  136.6 3.1 copy-start.4
  146.9 2.1 copy-start.2
  146.9 2.6 copy-start.6
  146.9 3.4 copy-start.8
  210.5 3.4 copy-start.20
  210.5 281.3 %copy-start.25 = (pred[256]{0:T(512)(128)(4,1)S(1)}, pred[256]{0:T(512)(128)(4,1)}, u32[]{:S(2)}) copy-start(pred[256]{0:T(512)(128)(4,1)} %copy-done.24) | copy-start | bytes 772
  210.5 391.3 %all-gather.5.cloned.1.call-start = ((), (), s32[]{:S(2)}) async-start(), calls=%async_computation.4 | async-start | bytes 4718592 | tf_op jit(solution)/shard_map/all_gather | solution.py:97
  213.9 296.5 %copy-start.22 = (pred[256]{0:T(512)(128)(4,1)}, pred[256]{0:T(512)(128)(4,1)S(1)}, u32[]{:S(2)}) copy-start(pred[256]{0:T(512)(128)(4,1)S(1)} %iota_compare_fusion) | copy-start | bytes 772
  455.7 10.9 %collective-permute-start.4 = (f32[256,400]{1,0:T(8,128)}, f32[256,400]{1,0:T(8,128)S(1)}, u32[]{:S(2)}, u32[]{:S(2)}) collective-permute-start(f32[256,400]{1,0:T(8,128)} %param.11), channel_id=1, source_target_pairs={{0,8},{8,0},{16,24},{24,16},{32,40},{40,32},{48,56},{56,48},{64,72... | collective-permute-start | bytes 1228808 | tf_op jit(solution)/shard_map/cond/branch_1_fun/ppermute | solution.py:21
  467.4 11.9 %collective-permute-start.6 = (f32[256,400]{1,0:T(8,128)}, f32[256,400]{1,0:T(8,128)S(1)}, u32[]{:S(2)}, u32[]{:S(2)}) collective-permute-start(f32[256,400]{1,0:T(8,128)} %param.15), channel_id=1, source_target_pairs={{0,32},{32,0},{8,40},{40,8},{16,48},{48,16},{24,56},{56,24},{64,96... | collective-permute-start | bytes 1228808 | tf_op jit(solution)/shard_map/cond/branch_1_fun/ppermute | solution.py:21
  480.1 10.9 %collective-permute-start.7 = (f32[256,400]{1,0:T(8,128)}, f32[256,400]{1,0:T(8,128)S(1)}, u32[]{:S(2)}, u32[]{:S(2)}) collective-permute-start(f32[256,400]{1,0:T(8,128)} %param.17), channel_id=1, source_target_pairs={{0,64},{64,0},{8,72},{72,8},{16,80},{80,16},{24,88},{88,24},{32,96... | collective-permute-start | bytes 1228808 | tf_op jit(solution)/shard_map/cond/branch_1_fun/ppermute | solution.py:21
  498.6 3.3 copy-start.14
  498.6 3.5 copy-start
  501.4 0.6 copy-start.12
  510.5 14.2 %collective-permute-start.8 = (f32[256,400]{1,0:T(8,128)S(1)}, f32[256,400]{1,0:T(8,128)S(1)}, u32[]{:S(2)}, u32[]{:S(2)}) collective-permute-start(f32[256,400]{1,0:T(8,128)S(1)} %param.19), channel_id=1, source_target_pairs={{0,8},{8,0},{16,24},{24,16},{32,40},{40,32},{48,56},{56,48},{64,72... | collective-permute-start | bytes 1228808 | tf_op jit(solution)/shard_map/cond/branch_1_fun/ppermute | solution.py:21
  524.8 10.9 %collective-permute-start.9 = (f32[256,400]{1,0:T(8,128)S(1)}, f32[256,400]{1,0:T(8,128)S(1)}, u32[]{:S(2)}, u32[]{:S(2)}) collective-permute-start(f32[256,400]{1,0:T(8,128)S(1)} %param.21), channel_id=1, source_target_pairs={{0,16},{16,0},{8,24},{24,8},{32,48},{48,32},{40,56},{56,40},{64,80... | collective-permute-start | bytes 1228808 | tf_op jit(solution)/shard_map/cond/branch_1_fun/ppermute | solution.py:21
  535.7 13.8 %collective-permute-start.10 = (f32[256,400]{1,0:T(8,128)S(1)}, f32[256,400]{1,0:T(8,128)S(1)}, u32[]{:S(2)}, u32[]{:S(2)}) collective-permute-start(f32[256,400]{1,0:T(8,128)S(1)} %param.23), channel_id=1, source_target_pairs={{0,32},{32,0},{8,40},{40,8},{16,48},{48,16},{24,56},{56,24},{64,96... | collective-permute-start | bytes 1228808 | tf_op jit(solution)/shard_map/cond/branch_1_fun/ppermute | solution.py:21
  549.6 10.8 %collective-permute-start.11 = (f32[256,400]{1,0:T(8,128)S(1)}, f32[256,400]{1,0:T(8,128)S(1)}, u32[]{:S(2)}, u32[]{:S(2)}) collective-permute-start(f32[256,400]{1,0:T(8,128)S(1)} %param.25), channel_id=1, source_target_pairs={{0,64},{64,0},{8,72},{72,8},{16,80},{80,16},{24,88},{88,24},{32,96... | collective-permute-start | bytes 1228808 | tf_op jit(solution)/shard_map/cond/branch_1_fun/ppermute | solution.py:21
  560.4 0.8 copy-start.11
  561.2 420.7 %reduce-scatter.5.cloned.1.call-start = ((), (), s32[]{:S(2)}) async-start(), calls=%async_computation.5 | async-start | bytes 4718592 | tf_op jit(solution)/shard_map/reduce_scatter | solution.py:132
  665.0 3.1 copy-start.5
  675.2 2.1 copy-start.3
  675.3 2.6 copy-start.7
  675.3 3.4 copy-start.9
  733.8 297.8 %copy-start.23 = (pred[256]{0:T(512)(128)(4,1)S(1)}, pred[256]{0:T(512)(128)(4,1)}, u32[]{:S(2)}) copy-start(pred[256]{0:T(512)(128)(4,1)} %copy-done.22) | copy-start | bytes 772
  981.9 10.9 %collective-permute-start.12 = (f32[256,400]{1,0:T(8,128)}, f32[256,400]{1,0:T(8,128)S(1)}, u32[]{:S(2)}, u32[]{:S(2)}) collective-permute-start(f32[256,400]{1,0:T(8,128)} %param.29), channel_id=1, source_target_pairs={{0,8},{8,0},{16,24},{24,16},{32,40},{40,32},{48,56},{56,48},{64,72... | collective-permute-start | bytes 1228808 | tf_op jit(solution)/shard_map/cond/branch_1_fun/ppermute | solution.py:21
  993.7 12.6 %collective-permute-start.13 = (f32[256,400]{1,0:T(8,128)}, f32[256,400]{1,0:T(8,128)S(1)}, u32[]{:S(2)}, u32[]{:S(2)}) collective-permute-start(f32[256,400]{1,0:T(8,128)} %param.31), channel_id=1, source_target_pairs={{0,16},{16,0},{8,24},{24,8},{32,48},{48,32},{40,56},{56,40},{64,80... | collective-permute-start | bytes 1228808 | tf_op jit(solution)/shard_map/cond/branch_1_fun/ppermute | solution.py:21
  1007.1 12.0 %collective-permute-start.14 = (f32[256,400]{1,0:T(8,128)}, f32[256,400]{1,0:T(8,128)S(1)}, u32[]{:S(2)}, u32[]{:S(2)}) collective-permute-start(f32[256,400]{1,0:T(8,128)} %param.33), channel_id=1, source_target_pairs={{0,32},{32,0},{8,40},{40,8},{16,48},{48,16},{24,56},{56,24},{64,96... | collective-permute-start | bytes 1228808 | tf_op jit(solution)/shard_map/cond/branch_1_fun/ppermute | solution.py:21
  1019.9 10.9 %collective-permute-start.15 = (f32[256,400]{1,0:T(8,128)}, f32[256,400]{1,0:T(8,128)S(1)}, u32[]{:S(2)}, u32[]{:S(2)}) collective-permute-start(f32[256,400]{1,0:T(8,128)} %param.35), channel_id=1, source_target_pairs={{0,64},{64,0},{8,72},{72,8},{16,80},{80,16},{24,88},{88,24},{32,96... | collective-permute-start | bytes 1228808 | tf_op jit(solution)/shard_map/cond/branch_1_fun/ppermute | solution.py:21
  1031.6 9.6 copy-start.15
  1038.5 2.7 copy-start.13
  1038.5 3.5 copy-start.1
Sparse Core Ops, SparseCore 0:
  62.0 33.3 all-gather.2
  210.7 244.9 reduce-scatter.2
  561.3 40.4 all-gather.4
  734.0 247.9 reduce-scatter.4
where the time goes:
time: 1080 us; the launch traced here: 1060 us
  waiting for transfers between devices  700 us (65%)
  local copies, waits for them, and re-layouts  137 us (13%)
  other arithmetic  110 us (10%)
  matrix products  46.6 us (4%)
  loops' own time  29.5 us (3%)
  between operations  19.7 us (2%)
  starting transfers between devices  16.1 us (1%)
    reduce_scatter x2, waiting for transfers between devices, body(): lax.psum_scatter(block_grad, 'sub', scatter_dimension=0, tiled=True)  490 us
    ppermute x14, waiting for transfers between devices, partner_2(): return lax.ppermute(block, axis, route)  154 us
    all_gather x2, waiting for transfers between devices, body(): partner_block = lax.all_gather(incoming, 'sub', axis=0, tiled=True)  56.6 us
    scatter-add x4, other arithmetic, step(): block_grad.at[tail_part].add(tail_grad).at[negative_part].add(negative_grad)  45.7 us
    another operation x2, loops' own time, body(): lax.fori_loop(0, group_counts[round_number, 0], step, (empty_rows, empty_...  29.4 us
    scatter-add x2, other arithmetic, step(): rows_grad = rows_grad.at[head_part].add(head_grad)  22.9 us
    gather x4, local copies, waits for them, and re-layouts, group_terms(): scale_rows = relations[relation_part]  22.6 us
  transfers between devices with their start and end apart: 18, of which 18 were waited for; matrix products, arithmetic and copies ran while one was open for 2% of the time, Pallas kernels for 0%

commit v1 on v0

v1 whole, which is shorter than its diff:
```python
import jax
import jax.numpy as jnp
from jax import lax
from jax.experimental import pallas as pl
from jax.experimental.pallas import tpu as pltpu
from jax.sharding import PartitionSpec as P

F32 = jnp.float32
BF16 = jnp.bfloat16
LOG2E = 1.4426950408889634
LEARN_RATE = 0.1

D = 400
FULL = 384
TAIL = D - FULL
GROUP = 1000
GPAD = 1024
LIST = 256
SUBS = 8
SLOTS = SUBS * LIST
KCAT = 3 * FULL + 128
VMEM_LIMIT = 60 * 1024 * 1024

VSPEC = pl.BlockSpec(memory_space=pltpu.VMEM)
SSPEC = pl.BlockSpec(memory_space=pltpu.SMEM)


def split2(x):
    high = x.astype(BF16)
    return high, (x - high.astype(F32)).astype(BF16)


def split3(x):
    high, rest = split2(x)
    low = x - high.astype(F32) - rest.astype(F32)
    return high, rest, low.astype(BF16)


def dot(a, b):
    return lax.dot_general(a, b, (((1,), (0,)), ((), ())), preferred_element_type=F32)


def dot_nt(a, b):
    return lax.dot_general(a, b, (((1,), (1,)), ((), ())), preferred_element_type=F32)


def params(**more):
    return pltpu.CompilerParams(vmem_limit_bytes=VMEM_LIMIT, **more)


def cost(flops, moved):
    return pl.CostEstimate(flops=int(flops), bytes_accessed=int(moved), transcendentals=0)


def pack_rows(source, target, start, target_start):
    for j in range(4):
        if j < 3:
            tile = source[128 * j : 128 * (j + 1), pl.ds(start, 128)]
        else:
            tile = jnp.concatenate(
                [source[FULL:D, pl.ds(start, 128)], jnp.zeros((128 - TAIL, 128), F32)], axis=0
            )
        target[pl.ds(target_start + j, 128, stride=4), :] = tile.T


def relation_kernel(ids, table_t, out, packed):
    half = table_t.shape[1]
    step = pl.program_id(0)
    first = step * half

    @pl.loop(0, half // 128)
    def _(i):
        start = pl.multiple_of(i * 128, 128)
        pack_rows(table_t, packed, start, (first + start) * 4)

    @pl.when(step == pl.num_programs(0) - 1)
    def _():
        rounds, edges = ids.shape

        for r in range(rounds):

            @pl.loop(0, edges // 8)
            def _(i):
                for u in range(8):
                    e = i * 8 + u
                    row = pl.multiple_of(ids[r, e] * 4, 4)
                    at = pl.multiple_of(e * 4, 4)
                    out[r, pl.ds(at, 4), :] = packed[pl.ds(row, 4), :]


def gather_relations(relation_ids, relations_t):
    rounds, edges = relation_ids.shape
    count = relations_t.shape[1]
    half = count // 2
    return pl.pallas_call(
        relation_kernel,
        grid=(2,),
        in_specs=[SSPEC, pl.BlockSpec((D, half), lambda i: (0, i))],
        out_specs=pl.BlockSpec((rounds, edges * 4, 128), lambda i: (0, 0, 0)),
        out_shape=jax.ShapeDtypeStruct((rounds, edges * 4, 128), F32),
        scratch_shapes=[pltpu.VMEM((count * 4, 128), F32)],
        compiler_params=params(),
        cost_estimate=cost(2e9, 60e6),
        name="relation_rows",
    )(relation_ids, relations_t)


def pick_columns(table_t, ids_row, count):
    rows = table_t.shape[1]
    slot = lax.broadcasted_iota(jnp.int32, ids_row.shape, 1)
    wanted = jnp.where(slot < count, ids_row, -1)
    row = lax.broadcasted_iota(jnp.int32, (rows, LIST), 0)
    onehot = jnp.where(row == wanted, 1.0, 0.0).astype(BF16)
    high, mid, low = split3(table_t)
    return dot(high, onehot) + dot(mid, onehot) + dot(low, onehot)


def sent_kernel(counts, ids, table_t, out):
    out[...] = pick_columns(table_t[...], ids[0:1, :], counts[0, 0])


def first_sent(row_counts, row_lists, table_t):
    return pl.pallas_call(
        sent_kernel,
        in_specs=[SSPEC, VSPEC, VSPEC],
        out_specs=VSPEC,
        out_shape=jax.ShapeDtypeStruct((D, LIST), F32),
        compiler_params=params(),
        name="sent_rows",
    )(row_counts, row_lists, table_t)


def query_kernel(round_number, ids, table_t, scale, cat, flipped, table, packed):
    groups = cat.shape[0]

    @pl.loop(0, table_t.shape[1] // 128)
    def _(i):
        start = pl.multiple_of(i * 128, 128)
        pack_rows(table_t, table, start, start * 4)

    for g in range(groups):

        @pl.loop(0, GROUP // 8)
        def _(i):
            for u in range(8):
                e = i * 8 + u
                row = pl.multiple_of(ids[round_number, g * GROUP + e] * 4, 4)
                at = pl.multiple_of(e * 4, 4)
                scaled = pl.multiple_of((g * GROUP + e) * 4, 4)
                packed[pl.ds(at, 4), :] = table[pl.ds(row, 4), :] * scale[0, pl.ds(scaled, 4), :]

        packed[4 * GROUP :, :] = jnp.zeros((4 * (GPAD - GROUP), 128), F32)

        @pl.loop(0, GPAD // 128)
        def _(b):
            rows = pl.ds(pl.multiple_of(b * 128, 128), 128)
            for j in range(4):
                tile = packed[pl.ds(b * 512 + j, 128, stride=4), :]
                high, low = split2(tile * LOG2E)
                if j < 3:
                    cat[g, rows, 128 * j : 128 * (j + 1)] = high
                    cat[g, rows, FULL + 128 * j : FULL + 128 * (j + 1)] = high
                    cat[g, rows, 2 * FULL + 128 * j : 2 * FULL + 128 * (j + 1)] = low
                else:
                    high, low = high.astype(F32), low.astype(F32)
                    both = high + pltpu.roll(high, TAIL, 1) + pltpu.roll(low, 2 * TAIL, 1)
                    cat[g, rows, 3 * FULL :] = both.astype(BF16)
                high, low = split2(tile.T)
                width = 128 if j < 3 else TAIL
                flipped[g, 128 * j : 128 * j + width, rows] = high[:width]
                flipped[g, D + 128 * j : D + 128 * j + width, rows] = low[:width]


def make_queries(round_number, head_ids, table_t, scale, groups):
    def kernel(*refs):
        query_kernel(round_number, *refs)

    edges = scale.shape[1]
    return pl.pallas_call(
        kernel,
        grid=(1,),
        in_specs=[SSPEC, VSPEC, pl.BlockSpec((1, edges, 128), lambda i: (round_number, 0, 0))],
        out_specs=[VSPEC, VSPEC],
        out_shape=[
            jax.ShapeDtypeStruct((groups, GPAD, KCAT), BF16),
            jax.ShapeDtypeStruct((groups, 2 * D, GPAD), BF16),
        ],
        scratch_shapes=[
            pltpu.VMEM((table_t.shape[1] * 4, 128), F32),
            pltpu.VMEM((GPAD * 4, 128), F32),
        ],
        compiler_params=params(),
        cost_estimate=cost(2e9, 40e6),
        name="queries",
    )(head_ids, table_t, scale)


def score_kernel(
    round_number, counts, cat, flipped, block, tails, negatives, share, block_grad,
    block_cat, scores, tail_columns, bias,
):
    g = pl.program_id(0)

    @pl.when(g == 0)
    def _():
        @pl.loop(0, SUBS)
        def _(s):
            high, low = split2(block[s])
            block_cat[s, 0:FULL, :] = high[:FULL]
            block_cat[s, FULL : 2 * FULL, :] = low[:FULL]
            block_cat[s, 2 * FULL : 3 * FULL, :] = high[:FULL]
            block_cat[s, 3 * FULL : 3 * FULL + TAIL, :] = high[FULL:]
            block_cat[s, 3 * FULL + TAIL : 3 * FULL + 2 * TAIL, :] = low[FULL:]
            block_cat[s, 3 * FULL + 2 * TAIL : 3 * FULL + 3 * TAIL, :] = high[FULL:]
            block_cat[s, 3 * FULL + 3 * TAIL :, :] = jnp.zeros((128 - 3 * TAIL, LIST), BF16)
            block_grad[s] = jnp.zeros((D, LIST), F32)

    @pl.when(g < counts[round_number, 0])
    def _():
        @pl.loop(0, SUBS)
        def _(s):
            at = pl.ds(pl.multiple_of(s * LIST, LIST), LIST)
            scores[:, at] = dot(cat[0], block_cat[s])

        drawn = negatives[0, 0]
        total = jnp.zeros((16, 128), F32)
        low_iota = lax.broadcasted_iota(jnp.int32, (128, 128), 0)
        high_iota = lax.broadcasted_iota(jnp.int32, (16, 128), 0)
        for b in range(GPAD // 128):
            row = drawn[b : b + 1, :]
            low_hot = jnp.where(low_iota == jnp.bitwise_and(row, 127), 1.0, 0.0).astype(BF16)
            high_hot = jnp.where(high_iota == jnp.right_shift(row, 7), 1.0, 0.0).astype(BF16)
            total = total + dot_nt(high_hot, low_hot)
        bias[...] = jnp.where(total > 0.5, jnp.log2(jnp.maximum(total, 1.0)), -1e30)

        tail = tails[0, 0].astype(F32)
        for b in range(GPAD // 128):
            tail_columns[128 * b : 128 * (b + 1), :] = jnp.broadcast_to(tail[b : b + 1, :], (128, 128)).T

        rows_here = 16
        lane = lax.broadcasted_iota(jnp.int32, (rows_here, 128), 1).astype(F32)
        row_iota = lax.broadcasted_iota(jnp.int32, (rows_here, 1), 0)
        tiles = SLOTS // 128

        @pl.loop(0, GPAD // rows_here, unroll=2)
        def _(i):
            first = pl.multiple_of(i * rows_here, rows_here)
            rows = pl.ds(first, rows_here)
            offset = tail_columns[rows, :] - lane
            own = None
            shifted = []
            top = None
            for j in range(tiles):
                raw = scores[rows, 128 * j : 128 * (j + 1)]
                hit = jnp.where(offset == 128.0 * j, raw, 0.0)
                own = hit if own is None else own + hit
                moved = raw + bias[j : j + 1, :]
                shifted.append(moved)
                top = moved if top is None else jnp.maximum(top, moved)
            positive = jnp.sum(own, axis=1, keepdims=True)
            top = jnp.maximum(jnp.max(top, axis=1, keepdims=True), positive)
            total = None
            weights = []
            for j in range(tiles):
                weight = jnp.exp2(shifted[j] - top)
                weights.append(weight)
                total = weight if total is None else total + weight
            negative_sum = jnp.sum(total, axis=1, keepdims=True)
            active = jnp.where(row_iota + first < GROUP, 1.0, 0.0)
            inverse = active / (jnp.exp2(positive - top) + negative_sum)
            own_share = -negative_sum * inverse
            for j in range(tiles):
                value = weights[j] * inverse + jnp.where(offset == 128.0 * j, own_share, 0.0)
                high, low = split2(value)
                share[0, 0, rows, 128 * j : 128 * (j + 1)] = high
                share[0, 1, rows, 128 * j : 128 * (j + 1)] = low

        @pl.loop(0, SUBS)
        def _(s):
            at = pl.ds(pl.multiple_of(s * LIST, LIST), LIST)
            both = dot(flipped[0], share[0, 0, :, at])
            cross = dot(flipped[0, :D, :], share[0, 1, :, at])
            block_grad[s] += both[:D] + both[D:] + cross


def score_groups(round_number, group_counts, cat, flipped, block, tails, negatives):
    def kernel(*refs):
        score_kernel(round_number, *refs)

    groups = cat.shape[0]
    return pl.pallas_call(
        kernel,
        grid=(groups,),
        in_specs=[
            SSPEC,
            pl.BlockSpec((1, GPAD, KCAT), lambda g: (g, 0, 0)),
            pl.BlockSpec((1, 2 * D, GPAD), lambda g: (g, 0, 0)),
            VSPEC,
            pl.BlockSpec((1, 1, 8, 128), lambda g: (round_number, g, 0, 0)),
            pl.BlockSpec((1, 1, 8, 128), lambda g: (round_number, g, 0, 0)),
        ],
        out_specs=[pl.BlockSpec((1, 2, GPAD, SLOTS), lambda g: (g, 0, 0, 0)), VSPEC],
        out_shape=[
            jax.ShapeDtypeStruct((groups, 2, GPAD, SLOTS), BF16),
            jax.ShapeDtypeStruct((SUBS, D, LIST), F32),
        ],
        scratch_shapes=[
            pltpu.VMEM((SUBS, KCAT, LIST), BF16),
            pltpu.VMEM((GPAD, SLOTS), F32),
            pltpu.VMEM((GPAD, 128), F32),
            pltpu.VMEM((16, 128), F32),
        ],
        compiler_params=params(),
        cost_estimate=cost(40e9, 60e6),
        name="scores",
    )(group_counts, cat, flipped, block, tails, negatives)


def head_kernel(
    round_number, counts, ids, share, block, scale, out, rows_high, rows_low, grad, packed, *sums
):
    g = pl.program_id(0)
    parts = len(sums)

    @pl.when(g == 0)
    def _():
        @pl.loop(0, SUBS)
        def _(s):
            for h in range(LIST // 128):
                rows = pl.ds(pl.multiple_of(s * LIST + h * 128, 128), 128)
                for j in range(4):
                    if j < 3:
                        tile = block[s, 128 * j : 128 * (j + 1), 128 * h : 128 * (h + 1)]
                    else:
                        tile = jnp.concatenate(
                            [
                                block[s, FULL:D, 128 * h : 128 * (h + 1)],
                                jnp.zeros((128 - TAIL, 128), F32),
                            ],
                            axis=0,
                        )
                    high, low = split2(tile.T)
                    rows_high[rows, 128 * j : 128 * (j + 1)] = high
                    rows_low[rows, 128 * j : 128 * (j + 1)] = low

        for part in sums:
            part[...] = jnp.zeros_like(part)

    @pl.when(g < counts[round_number, 0])
    def _():
        for n in range(2):
            at = slice(256 * n, 256 * (n + 1))
            grad[...] = (
                dot(share[0, 0], rows_high[:, at])
                + dot(share[0, 0], rows_low[:, at])
                + dot(share[0, 1], rows_high[:, at])
            )
            for h in range(2):
                for b in range(GPAD // 128):
                    packed[pl.ds(512 * b + 2 * n + h, 128, stride=4), :] = grad[
                        128 * b : 128 * (b + 1), 128 * h : 128 * (h + 1)
                    ]

        base = g * GROUP

        @pl.loop(0, GROUP // parts, unroll=2)
        def _(i):
            news = []
            for u in range(parts):
                e = i * parts + u
                row = pl.ds(pl.multiple_of(ids[round_number, base + e] * 4, 4), 4)
                at = pl.ds(pl.multiple_of(e * 4, 4), 4)
                term = packed[at, :] * scale[0, at, :]
                news.append((row, sums[u][row, :] + term))
            for u in range(parts):
                row, value = news[u]
                sums[u][row, :] = value

    @pl.when(g == pl.num_programs(0) - 1)
    def _():
        @pl.loop(0, out.shape[1] // 128)
        def _(i):
            columns = pl.ds(pl.multiple_of(i * 128, 128), 128)
            for j in range(4):
                at = pl.ds(i * 512 + j, 128, stride=4)
                tile = sums[0][at, :]
                for part in sums[1:]:
                    tile = tile + part[at, :]
                width = 128 if j < 3 else TAIL
                out[128 * j : 128 * j + width, columns] = tile.T[:width]


def head_gradients(round_number, group_counts, head_ids, share, block, scale, rows):
    def kernel(*refs):
        head_kernel(round_number, *refs)

    groups = share.shape[0]
    parts = 4
    return pl.pallas_call(
        kernel,
        grid=(groups,),
        in_specs=[
            SSPEC,
            SSPEC,
            pl.BlockSpec((1, 2, GPAD, SLOTS), lambda g: (g, 0, 0, 0)),
            VSPEC,
            pl.BlockSpec((1, GROUP * 4, 128), lambda g: (round_number, g, 0)),
        ],
        out_specs=VSPEC,
        out_shape=jax.ShapeDtypeStruct((D, rows), F32),
        scratch_shapes=[
            pltpu.VMEM((SLOTS, 512), BF16),
            pltpu.VMEM((SLOTS, 512), BF16),
            pltpu.VMEM((GPAD, 256), F32),
            pltpu.VMEM((GPAD * 4, 128), F32),
        ]
        + [pltpu.VMEM((rows * 4, 128), F32)] * parts,
        compiler_params=params(),
        cost_estimate=cost(20e9, 60e6),
        name="head_gradients",
    )(group_counts, head_ids, share, block, scale)


def adagrad_kernel(
    round_number, last, counts, ids, ids_column, head_grad, returned, table_t, state,
    new_table_t, new_state, *sent,
):
    rows = table_t.shape[1]
    width = 512
    wanted = ids_column[round_number]
    slot = lax.broadcasted_iota(jnp.int32, wanted.shape, 0)
    wanted = jnp.where(slot < counts[round_number, 0], wanted, -1)
    high, mid, low = split3(returned[...])
    for first in range(0, rows, width):
        at = slice(first, first + width)
        row = lax.broadcasted_iota(jnp.int32, (LIST, width), 1) + first
        onehot = jnp.where(row == wanted, 1.0, 0.0).astype(BF16)
        totals = head_grad[:, at] + (dot(high, onehot) + dot(mid, onehot) + dot(low, onehot))
        fresh = state[:, at] + jnp.sum(totals * totals, axis=0, keepdims=True) / D
        new_state[:, at] = fresh
        new_table_t[:, at] = table_t[:, at] - LEARN_RATE * totals / jnp.sqrt(fresh)
    if not last:
        sent[0][...] = pick_columns(
            new_table_t[...], ids[round_number + 1 : round_number + 2, :], counts[round_number + 1, 0]
        )


def adagrad(round_number, last, row_counts, row_lists, ids_column, head_grad, returned, table_t, state):
    def kernel(*refs):
        adagrad_kernel(round_number, last, *refs)

    outs = [jax.ShapeDtypeStruct(table_t.shape, F32), jax.ShapeDtypeStruct(state.shape, F32)]
    if not last:
        outs.append(jax.ShapeDtypeStruct((D, LIST), F32))
    return pl.pallas_call(
        kernel,
        in_specs=[SSPEC] + [VSPEC] * 6,
        out_specs=[VSPEC] * len(outs),
        out_shape=outs,
        compiler_params=params(),
        name="adagrad",
    )(row_counts, row_lists, ids_column, head_grad, returned, table_t, state)


def swap_partner(values, mask):
    count = lax.axis_size("dom")

    def branch(m):
        route = [(i, i ^ m) for i in range(count)]
        return lambda held: lax.ppermute(held, "dom", route)

    return lax.switch(mask - 1, [branch(m) for m in range(1, count)], values)


def body(
    embeddings,
    adagrad_state,
    relations,
    pairing,
    row_lists,
    row_counts,
    group_counts,
    head_ids,
    relation_ids,
    tail_slots,
    negatives,
):
    rounds = pairing.shape[0]
    rows = embeddings.shape[0]
    groups = head_ids.shape[1] // GROUP
    table_t = embeddings.T
    state = adagrad_state.reshape(1, rows)
    ids_column = row_lists.reshape(rounds, LIST, 1)

    def lanes(ids):
        ids = ids.reshape(rounds, groups, GROUP)
        ids = jnp.pad(ids, ((0, 0), (0, 0), (0, GPAD - GROUP)), constant_values=-1)
        return ids.reshape(rounds, groups, GPAD // 128, 128)

    tails = lanes(tail_slots)
    drawn = lanes(negatives)
    sent = first_sent(row_counts, row_lists, table_t)
    scale = gather_relations(relation_ids, relations.T)
    for r in range(rounds):
        incoming = swap_partner(sent, pairing[r])
        block = lax.all_gather(incoming, "sub", axis=0, tiled=False)
        cat, flipped = make_queries(r, head_ids, table_t, scale, groups)
        share, block_grad = score_groups(r, group_counts, cat, flipped, block, tails, drawn)
        own_share = lax.psum_scatter(block_grad, "sub", scatter_dimension=0, tiled=False)
        head_grad = head_gradients(r, group_counts, head_ids, share, block, scale, rows)
        returned = swap_partner(own_share, pairing[r])
        last = r == rounds - 1
        done = adagrad(r, last, row_counts, row_lists, ids_column, head_grad, returned, table_t, state)
        table_t, state = done[0], done[1]
        if not last:
            sent = done[2]
    return (table_t.T, state.reshape(rows))


def solution(mesh):
    in_specs = (
        P(("dom", "sub"), None),
        P(("dom", "sub")),
        P(),
        P(),
        P(None, ("dom", "sub")),
        P(None, ("dom", "sub")),
        P(None, ("dom", "sub")),
        P(None, ("dom", "sub")),
        P(None, ("dom", "sub")),
        P(None, ("dom", "sub")),
        P(None, ("dom", "sub")),
    )
    out_specs = (P(("dom", "sub"), None), P(("dom", "sub")))
    return jax.shard_map(body, mesh=mesh, in_specs=in_specs, out_specs=out_specs, check_vma=False)
```

time: 1080 us -> 425 us (0.39); the launches traced: 1060 us -> 419 us
  waiting for transfers between devices: 700 us -> 80.3 us
  Pallas kernels: 0 us -> 306 us
  local copies, waits for them, and re-layouts: 137 us -> 5.63 us
  other arithmetic: 110 us -> 0 us
  matrix products: 46.6 us -> 0 us
  loops' own time: 29.5 us -> 0.22 us
    reduce_scatter x2, waiting for transfers between devices: 490 us -> 24.2 us  [body(): lax.psum_scatter(block_grad, 'sub', scatter_dimension=0, tiled=False)]
    pallas_call x0 -> x10, Pallas kernels: none -> 306 us  [the longest x2 134 us: score_groups(): pl.pallas_call(kernel, grid=(groups,), in_specs=[SSPEC, pl.BlockSpec((1,...]
    ppermute x14 -> x4, waiting for transfers between devices: 154 us -> 45.4 us  [branch(): return lambda held: lax.ppermute(held, 'dom', route)]
    scatter-add x8 -> x0, other arithmetic: 82.4 us -> none  [the longest x4 45.7 us: step(): block_grad.at[tail_part].add(tail_grad).at[negative_part].add(negative_grad)]
    gather x16 -> x0, local copies, waits for them, and re-layouts: 76.7 us -> none  [the longest x4 22.6 us: group_terms(): scale_rows = relations[relation_part]]
    dot_general x6 -> x0, matrix products: 46.6 us -> none  [the longest x2 19.6 us: group_terms(): jnp.dot(neg_share.T, queries, precision=exact_mode, preferred_element_typ...]
    all_gather x2, waiting for transfers between devices: 56.6 us -> 10.6 us  [body(): block = lax.all_gather(incoming, 'sub', axis=0, tiled=False)]
    another operation x18 -> x4, loops' own time: 29.5 us -> 0.22 us  [swap_partner(): return lax.switch(mask - 1, [branch(m) for m in range(1, count)], values)]
  transfers between devices with their start and end apart: 18 -> 8, of which waited for: 18 -> 6; matrix products, arithmetic and copies ran while one was open for 2% -> 1% of each run, Pallas kernels for 0% -> 37%
where the time goes in v1:
time: 425 us; the launch traced here: 419 us
  Pallas kernels  306 us (72%)
  waiting for transfers between devices  80.3 us (19%)
  between operations  15.4 us (4%)
  starting transfers between devices  11 us (3%)
  local copies, waits for them, and re-layouts  5.63 us (1%)
    pallas_call x2, Pallas kernels, score_groups(): pl.pallas_call(kernel, grid=(groups,), in_specs=[SSPEC, pl.BlockSpec((1,...  134 us
    pallas_call x2, Pallas kernels, head_gradients(): pl.pallas_call(kernel, grid=(groups,), in_specs=[SSPEC, SSPEC, pl.BlockSp...  73.3 us
    pallas_call x2, Pallas kernels, make_queries(): pl.pallas_call(kernel, grid=(1,), in_specs=[SSPEC, VSPEC, pl.BlockSpec((1...  47.6 us
    ppermute x4, waiting for transfers between devices, branch(): return lambda held: lax.ppermute(held, 'dom', route)  45.4 us
    pallas_call x1, Pallas kernels, gather_relations(): pl.pallas_call(relation_kernel, grid=(2,), in_specs=[SSPEC, pl.BlockSpec(...  32.2 us
    reduce_scatter x2, waiting for transfers between devices, body(): lax.psum_scatter(block_grad, 'sub', scatter_dimension=0, tiled=False)  24.2 us
    pallas_call x2, Pallas kernels, adagrad(): pl.pallas_call(kernel, in_specs=[SSPEC] + [VSPEC] * 6, out_specs=[VSPEC]...  15.5 us
    all_gather x2, waiting for transfers between devices, body(): block = lax.all_gather(incoming, 'sub', axis=0, tiled=False)  10.6 us
  transfers between devices with their start and end apart: 8, of which 6 were waited for; matrix products, arithmetic and copies ran while one was open for 1% of the time, Pallas kernels for 37%

profile of v1, /device:TPU:96, one launch (start us, length us, event | category | flops | bytes accessed | tf_op | source)
XLA Modules:
  0.0 418.6 jit_solution(3802540950851065145)
XLA Ops:
  7.2 0.0 copy-start.3
  7.2 0.0 copy-start.1
  7.2 0.0 copy-start.2
  7.2 0.0 all-gather.5.cloned.1.call-start
  7.2 1.3 copy.33.counts.refs_0_
  8.6 1.4 fusion
  10.6 3.5 sent_rows.1
  14.0 13.8 %conditional.4 = (f32[400,256]{1,0:T(8,128)}) conditional(s32[]{:T(128)} %bitcast.3, f32[400,256]{1,0:T(8,128)S(1)} %sent_rows.1, f32[400,256]{1,0:T(8,128)S(1)} %sent_rows.1, f32[400,256]{1,0:T(8,128)S(1)} %sent_rows.1, f32[400,256]{1,0:T(8,128)S(1)} %sent_rows.1, f32[400,256]{1,0:T(8,128)S(1)} %sent_rows.1, ...), branch_computations={%region_0.1_spmd, %region_1.2_spmd, %region_2.3_spmd, %region_3.4_... | conditional | bytes 1638448 | solution.py:472
  14.1 3.1 collective-permute-start.5
  17.2 10.7 %collective-permute-done.5 = f32[400,256]{1,0:T(8,128)} collective-permute-done((f32[400,256]{1,0:T(8,128)S(1)}, f32[400,256]{1,0:T(8,128)}, u32[]{:S(2)}, u32[]{:S(2)}) %collective-permute-start.5) | collective-permute-done | bytes 409632 | tf_op jit(solution)/shard_map/cond/branch_5_fun/ppermute | solution.py:470
  27.8 0.0 all-gather.5.cloned.1.call-update
  27.9 0.0 reduce-scatter.3.cloned.1.call-start
  27.9 0.0 copy-done.3
  27.9 0.6 copy.32.refs_0_
  28.6 0.0 copy-done.1
  28.6 0.1 reshape.36
  28.7 0.6 reshape.44.refs_4_
  29.3 0.0 copy-done.2
  29.3 0.1 reshape.38
  29.4 0.6 reshape.45.refs_5_
  30.0 32.2 %relation_rows.1.refs_2_.refs_4_ = f32[2,12000,128]{2,1,0:T(8,128)} custom-call(s32[2,3000]{1,0:T(2,128)} %ids.2, f32[400,7424]{1,0:T(8,128)} %bitcast.15), custom_call_target="tpu_custom_call" | custom-call | flops 2000000000 | bytes 60000000 | tf_op jit(solution)/shard_map/relation_rows/pallas_call | solution.py:95
  62.2 23.2 %queries.2 = (bf16[3,1024,1280]{2,1,0:T(8,128)(2,1)}, bf16[3,800,1024]{2,1,0:T(8,128)(2,1)}) custom-call(s32[2,3000]{1,0:T(2,128)} %refs_1_.6, f32[400,2048]{1,0:T(8,128)} %bitcast.13, f32[2,12000,128]{2,1,0:T(8,128)} %relation_rows.1.refs_2_.refs_4_), custom_call_target="tpu_custom_call" | custom-call | flops 2000000000 | bytes 40000000 | tf_op jit(solution)/shard_map/queries/pallas_call | solution.py:179
  85.4 0.0 all-gather.5.cloned.1.call-done
  85.4 57.0 %scores.2 = (bf16[3,2,1024,2048]{3,2,1,0:T(8,128)(2,1)}, f32[8,400,256]{2,1,0:T(8,128)}) custom-call(s32[2,1]{1,0:T(2,128)} %copy.32.refs_0_, bf16[3,1024,1280]{2,1,0:T(8,128)(2,1)} %get-tuple-element.139.refs_1_, bf16[3,800,1024]{2,1,0:T(8,128)(2,1)} %get-tuple-element.140.refs_2_, f32[8,400,256]{2,1,0:T(8,128)} %bitcast.18, ...), custom_call_target="tpu_custom_call" | custom-call | flops 40000000000 | bytes 60000000 | tf_op jit(solution)/shard_map/scores/pallas_call | solution.py:291
  142.4 0.0 reduce-scatter.3.cloned.1.call-update
  142.4 0.5 all-gather.7.cloned.1.call-start
  143.6 0.0 copy-done
  143.6 0.9 copy.34.refs_2_
  144.5 31.4 %head_gradients.2.refs_3_ = f32[400,2048]{1,0:T(8,128)} custom-call(s32[2,1]{1,0:T(2,128)} %copy.32.refs_0_, s32[2,3000]{1,0:T(2,128)} %refs_1_.6, bf16[3,2,1024,2048]{3,2,1,0:T(8,128)(2,1)} %get-tuple-element.141.refs_2_, f32[8,400,256]{2,1,0:T(8,128)} %bitcast.19, f32[2,12000,128]{2,1,0:T(8,128)} %relation_rows.1.refs_2_.refs_4_), custom_call_target="tpu_custom_call" | custom-call | flops 20000000000 | bytes 60000000 | tf_op jit(solution)/shard_map/head_gradients/pallas_call | solution.py:399
  175.9 24.2 %reduce-scatter.3.cloned.1.call-done = f32[1,400,256]{2,1,0:T(8,128)} async-done(((f32[8,400,256]{2,1,0:T(8,128)}), f32[1,400,256]{2,1,0:T(8,128)}) %reduce-scatter.3.cloned.1.call-update) | async-done | bytes 409616 | tf_op jit(solution)/shard_map/reduce_scatter | solution.py:509
  200.1 12.5 %conditional.5 = (f32[400,256]{1,0:T(8,128)}) conditional(s32[]{:T(128)} %bitcast.3, f32[400,256]{1,0:T(8,128)} %bitcast.23, f32[400,256]{1,0:T(8,128)} %bitcast.24, f32[400,256]{1,0:T(8,128)} %bitcast.25, f32[400,256]{1,0:T(8,128)} %bitcast.26, f32[400,256]{1,0:T(8,128)} %bitcast.27, ...), branch_computations={%region_16.17_spmd, %region_17.18_spmd, %region_18.19_spmd, %regio... | conditional | bytes 1638448 | solution.py:472
  200.1 3.3 collective-permute-start.20
  203.4 9.0 %collective-permute-done.20 = f32[400,256]{1,0:T(8,128)} collective-permute-done((f32[400,256]{1,0:T(8,128)}, f32[400,256]{1,0:T(8,128)}, u32[]{:S(2)}, u32[]{:S(2)}) %collective-permute-start.20) | collective-permute-done | bytes 409632 | tf_op jit(solution)/shard_map/cond/branch_5_fun/ppermute | solution.py:470
  212.6 8.5 %adagrad.2 = (f32[400,2048]{1,0:T(8,128)}, f32[1,2048]{1,0:T(1,128)}, f32[400,256]{1,0:T(8,128)S(1)}) custom-call(s32[2,1]{1,0:T(2,128)} %copy.33.counts.refs_0_, s32[2,256]{1,0:T(2,128)} %refs_1_.7, s32[2,256,1]{2,1,0:T(8,128)} %copy.34.refs_2_, f32[400,2048]{1,0:T(8,128)} %head_gradients.2.refs_3_, f32[400,256]{1,0:T(8,128)} %get-tuple-element.155.refs_4_, ...), custom_call_target="tpu_custom_call" | custom-call | tf_op jit(solution)/shard_map/adagrad/pallas_call | solution.py:455
  221.1 14.2 %conditional.6 = (f32[400,256]{1,0:T(8,128)}) conditional(s32[]{:T(128)} %bitcast.7, f32[400,256]{1,0:T(8,128)S(1)} %get-tuple-element.146, f32[400,256]{1,0:T(8,128)S(1)} %get-tuple-element.146, f32[400,256]{1,0:T(8,128)S(1)} %get-tuple-element.146, f32[400,256]{1,0:T(8,128)S(1)} %get-tuple-element.146, ...), branch_computations={%region_31.32_spmd, %region_32.33_spmd, %region_33.34_spmd, %regio... | conditional | bytes 1638448 | solution.py:472
  221.2 1.3 collective-permute-start.44
  222.4 12.9 %collective-permute-done.44 = f32[400,256]{1,0:T(8,128)} collective-permute-done((f32[400,256]{1,0:T(8,128)S(1)}, f32[400,256]{1,0:T(8,128)}, u32[]{:S(2)}, u32[]{:S(2)}) %collective-permute-start.44) | collective-permute-done | bytes 409632 | tf_op jit(solution)/shard_map/cond/branch_14_fun/ppermute | solution.py:470
  235.3 0.0 all-gather.7.cloned.1.call-update
  235.4 0.3 reduce-scatter.5.cloned.1.call-start
  235.6 24.4 %queries.3 = (bf16[3,1024,1280]{2,1,0:T(8,128)(2,1)}, bf16[3,800,1024]{2,1,0:T(8,128)(2,1)}) custom-call(s32[2,3000]{1,0:T(2,128)} %refs_1_.6, f32[400,2048]{1,0:T(8,128)} %get-tuple-element.143.refs_1_.refs_5_, f32[2,12000,128]{2,1,0:T(8,128)} %relation_rows.1.refs_2_.refs_4_), custom_call_target="tpu_custom_call" | custom-call | flops 2000000000 | bytes 40000000 | tf_op jit(solution)/shard_map/queries/pallas_call | solution.py:179
  260.0 10.6 %all-gather.7.cloned.1.call-done = f32[3200,256]{1,0:T(8,128)} async-done(((f32[400,256]{1,0:T(8,128)}), f32[3200,256]{1,0:T(8,128)}) %all-gather.7.cloned.1.call-update) | async-done | bytes 3276816 | tf_op jit(solution)/shard_map/all_gather | solution.py:506
  270.6 77.2 %scores.3 = (bf16[3,2,1024,2048]{3,2,1,0:T(8,128)(2,1)}, f32[8,400,256]{2,1,0:T(8,128)}) custom-call(s32[2,1]{1,0:T(2,128)} %copy.32.refs_0_, bf16[3,1024,1280]{2,1,0:T(8,128)(2,1)} %get-tuple-element.144.refs_1_, bf16[3,800,1024]{2,1,0:T(8,128)(2,1)} %get-tuple-element.145.refs_2_, f32[8,400,256]{2,1,0:T(8,128)} %bitcast.20, ...), custom_call_target="tpu_custom_call" | custom-call | flops 40000000000 | bytes 60000000 | tf_op jit(solution)/shard_map/scores/pallas_call | solution.py:291
  347.8 0.0 reduce-scatter.5.cloned.1.call-update
  347.8 41.8 %head_gradients.3.refs_3_ = f32[400,2048]{1,0:T(8,128)} custom-call(s32[2,1]{1,0:T(2,128)} %copy.32.refs_0_, s32[2,3000]{1,0:T(2,128)} %refs_1_.6, bf16[3,2,1024,2048]{3,2,1,0:T(8,128)(2,1)} %get-tuple-element.147.refs_2_, f32[8,400,256]{2,1,0:T(8,128)} %bitcast.21, f32[2,12000,128]{2,1,0:T(8,128)} %relation_rows.1.refs_2_.refs_4_), custom_call_target="tpu_custom_call" | custom-call | flops 20000000000 | bytes 60000000 | tf_op jit(solution)/shard_map/head_gradients/pallas_call | solution.py:399
  389.6 15.3 %conditional.7 = (f32[400,256]{1,0:T(8,128)}) conditional(s32[]{:T(128)} %bitcast.7, f32[400,256]{1,0:T(8,128)} %bitcast.38, f32[400,256]{1,0:T(8,128)} %bitcast.39, f32[400,256]{1,0:T(8,128)} %bitcast.40, f32[400,256]{1,0:T(8,128)} %bitcast.41, f32[400,256]{1,0:T(8,128)} %bitcast.42, ...), branch_computations={%region_47.48_spmd, %region_48.49_spmd, %region_49.50_spmd, %regio... | conditional | bytes 1638448 | solution.py:472
  389.6 2.5 collective-permute-start.59
  392.1 12.8 %collective-permute-done.59 = f32[400,256]{1,0:T(8,128)} collective-permute-done((f32[400,256]{1,0:T(8,128)}, f32[400,256]{1,0:T(8,128)}, u32[]{:S(2)}, u32[]{:S(2)}) %collective-permute-start.59) | collective-permute-done | bytes 409632 | tf_op jit(solution)/shard_map/cond/branch_14_fun/ppermute | solution.py:470
  404.9 7.0 %adagrad.3 = (f32[400,2048]{1,0:T(8,128)}, f32[1,2048]{1,0:T(1,128)}) custom-call(s32[2,1]{1,0:T(2,128)} %copy.33.counts.refs_0_, s32[2,256]{1,0:T(2,128)} %refs_1_.7, s32[2,256,1]{2,1,0:T(8,128)} %copy.34.refs_2_, f32[400,2048]{1,0:T(8,128)} %head_gradients.3.refs_3_, f32[400,256]{1,0:T(8,128)} %get-tuple-element.157.refs_4_, ...), custom_call_target="tpu_custom_call" | custom-call | tf_op jit(solution)/shard_map/adagrad/pallas_call | solution.py:455
  (4 shorter events, 0.0 us)
Async XLA Ops:
  7.2 20.8 %copy-start.3 = (s32[2,1]{0,1:T(1,128)S(1)}, s32[2,1]{0,1:T(1,128)}, u32[]{:S(2)}) copy-start(s32[2,1]{0,1:T(1,128)} %param.77) | copy-start | bytes 28
  7.2 21.4 %copy-start.1 = (s32[2,3000]{1,0:T(2,128)S(1)}, s32[2,3000]{1,0:T(2,128)}, u32[]{:S(2)}) copy-start(s32[2,3000]{1,0:T(2,128)} %param.80) | copy-start | bytes 72004
  7.2 22.1 %copy-start.2 = (s32[2,3000]{1,0:T(2,128)S(1)}, s32[2,3000]{1,0:T(2,128)}, u32[]{:S(2)}) copy-start(s32[2,3000]{1,0:T(2,128)} %param.81) | copy-start | bytes 72004
  7.2 78.2 %all-gather.5.cloned.1.call-start = ((), (), s32[]{:S(2)}) async-start(), calls=%async_computation.4 | async-start | bytes 3686400 | tf_op jit(solution)/shard_map/all_gather | solution.py:506
  14.1 13.8 %collective-permute-start.5 = (f32[400,256]{1,0:T(8,128)S(1)}, f32[400,256]{1,0:T(8,128)}, u32[]{:S(2)}, u32[]{:S(2)}) collective-permute-start(f32[400,256]{1,0:T(8,128)S(1)} %param.5), channel_id=1, source_target_pairs={{0,48},{8,56},{16,32},{24,40},{32,16},{40,24},{48,0},{56,8},{64,11... | collective-permute-start | bytes 1228808 | tf_op jit(solution)/shard_map/cond/branch_5_fun/ppermute | solution.py:470
  27.9 172.2 %reduce-scatter.3.cloned.1.call-start = ((), (), s32[]{:S(2)}) async-start(), calls=%async_computation.2 | async-start | bytes 3686400 | tf_op jit(solution)/shard_map/reduce_scatter | solution.py:509
  142.4 1.2 copy-start
  142.4 128.2 %all-gather.7.cloned.1.call-start = ((), (), s32[]{:S(2)}) async-start(), calls=%async_computation.5 | async-start | bytes 3686400 | tf_op jit(solution)/shard_map/all_gather | solution.py:506
  200.1 12.3 %collective-permute-start.20 = (f32[400,256]{1,0:T(8,128)}, f32[400,256]{1,0:T(8,128)}, u32[]{:S(2)}, u32[]{:S(2)}) collective-permute-start(f32[400,256]{1,0:T(8,128)} %param.20), channel_id=1, source_target_pairs={{0,48},{8,56},{16,32},{24,40},{32,16},{40,24},{48,0},{56,8},{64,11... | collective-permute-start | bytes 1228808 | tf_op jit(solution)/shard_map/cond/branch_5_fun/ppermute | solution.py:470
  221.2 14.2 %collective-permute-start.44 = (f32[400,256]{1,0:T(8,128)S(1)}, f32[400,256]{1,0:T(8,128)}, u32[]{:S(2)}, u32[]{:S(2)}) collective-permute-start(f32[400,256]{1,0:T(8,128)S(1)} %param.44), channel_id=1, source_target_pairs={{0,120},{8,112},{16,104},{24,96},{32,88},{40,80},{48,72},{56,64},{... | collective-permute-start | bytes 1228808 | tf_op jit(solution)/shard_map/cond/branch_14_fun/ppermute | solution.py:470
  235.4 154.3 %reduce-scatter.5.cloned.1.call-start = ((), (), s32[]{:S(2)}) async-start(), calls=%async_computation.3 | async-start | bytes 3686400 | tf_op jit(solution)/shard_map/reduce_scatter | solution.py:509
  389.6 15.3 %collective-permute-start.59 = (f32[400,256]{1,0:T(8,128)}, f32[400,256]{1,0:T(8,128)}, u32[]{:S(2)}, u32[]{:S(2)}) collective-permute-start(f32[400,256]{1,0:T(8,128)} %param.59), channel_id=1, source_target_pairs={{0,120},{8,112},{16,104},{24,96},{32,88},{40,80},{48,72},{56,64},{... | collective-permute-start | bytes 1228808 | tf_op jit(solution)/shard_map/cond/branch_14_fun/ppermute | solution.py:470
Sparse Core Ops, SparseCore 0:
  28.0 29.5 all-gather.4
  142.6 57.4 reduce-scatter.2
  235.5 35.1 all-gather.6
  348.0 35.8 reduce-scatter.4
